TPU v7x, 128 devices: a whole 4x4x4 slice. The times are simulated.
128 devices in a mesh: grp: 4 (over x_lo, core), dom: 32 (over y, x_hi, z).
Axes of the slice: x: 4 (x_hi: 2, x_lo: 2; x = x_hi * 2 + x_lo), y: 4, z: 4, core: 2. Of those that a mesh axis runs over, the one named last changes fastest.
Arguments:
- state: float32 [8192, 4, 72, 128], P(('grp', 'dom')), may hold values from -6 to 6
- neighbours: int32 [8192, 4], P(('grp', 'dom')), may hold values from 0 to 67, as said below
- remap_dest: int32 [65536], P(('grp', 'dom')), may hold values from 0 to 127, as said below
- remap_src: int32 [65536], P(('grp', 'dom')), may hold values from 0 to 63
- remap_block: int32 [65536], P(('grp', 'dom')), may hold values from 0 to 63
- remap_weights: float32 [65536, 128], P(('grp', 'dom')), may hold values from 0.2 to 1
- self_op: float32 [2, 128, 128], replicated, may hold values from -0.5 to 0.5
- edge_op: float32 [2, 128, 128], replicated, may hold values from -0.25 to 0.25
- vert_op: float32 [2, 72, 72], replicated, may hold values from -0.75 to 0.75
Outputs:
- new_state: float32 [8192, 4, 72, 128], P(('grp', 'dom'))
Inputs may be any that keep to these rules, and one draw needn't show every extreme that they name: Value v of local block b names local block v - 2 of the same device if 0 <= v - 2 < 64, else a block of the previous or next device along dom (wrapping); v lies between b and b + 4. The first two neighbours are the blocks b - 1 and b + 1. `remap_dest`: flat device index over grp and dom (grp slowest). Rows of an atmosphere device go to ocean devices, exactly 16 to each; rows of an ocean device go to atmosphere devices, exactly 16 to the atmosphere devices of each dom index together, at most 16 to any, exactly 16 to one.
All inputs are finite; a program needn't handle non-finite values.
Results may differ from a plain program's by a relative error of at most 0.0001.
Values sent between devices are 32-bit elements; how exact they have to be, the bound alone decides.
A program may use at most 192 MiB of HBM per device.

v0:
```python
import jax
import jax.numpy as jnp
from jax import lax
from jax.sharding import PartitionSpec as P

H = 2
SUBSTEPS = 2


def padded(cells, sides, width):
    for axis, dim in sides:
        count = lax.axis_size(axis)
        head = lax.slice_in_dim(cells, 0, width, axis=dim)
        tail = lax.slice_in_dim(cells, cells.shape[dim] - width, cells.shape[dim], axis=dim)
        cells = jnp.concatenate(
            [
                lax.ppermute(tail, axis, [(i, (i + 1) % count) for i in range(count)]),
                cells,
                lax.ppermute(head, axis, [((i + 1) % count, i) for i in range(count)]),
            ],
            axis=dim,
        )
    return cells


def advance_rows(center, nbrsum, self_m, edge_m, vert_m):
    lateral = center + 0.5 * (
        jnp.matmul(center, self_m, precision=lax.Precision.HIGHEST)
        + jnp.matmul(nbrsum, edge_m, precision=lax.Precision.HIGHEST)
    )
    return jnp.einsum("lm,bfmc->bflc", vert_m, lateral, precision=lax.Precision.HIGHEST)


def per_device(
    state, neighbours, remap_dest, remap_src, remap_block, remap_weights, self_op, edge_op, vert_op
):
    blocks = state.shape[0]
    levels = state.shape[2]
    slots = neighbours.shape[1]
    groups = lax.axis_size("grp")
    domains = lax.axis_size("dom")
    devices = groups * domains
    is_ocean = lax.axis_index("grp") == groups - 1
    comp = is_ocean.astype(jnp.int32)
    self_m = lax.dynamic_index_in_dim(self_op, comp, 0, keepdims=False)
    edge_m = lax.dynamic_index_in_dim(edge_op, comp, 0, keepdims=False)
    vert_m = lax.dynamic_index_in_dim(vert_op, comp, 0, keepdims=False)
    surf_level = jnp.where(is_ocean, 0, levels - 1).astype(jnp.int32)
    surface = lax.dynamic_index_in_dim(state[:, 0], surf_level, 1, keepdims=False)
    values = remap_weights * surface[remap_src]
    target = remap_dest * blocks + remap_block
    select = (target[:, None] == jnp.arange(devices * blocks, dtype=jnp.int32)[None, :]).astype(
        jnp.float32
    )
    dense = lax.dot_general(
        select, values, (((0,), (0,)), ((), ())), precision=lax.Precision.HIGHEST
    )
    received = lax.psum_scatter(dense, ("grp", "dom"), scatter_dimension=0, tiled=True)
    field = state
    for sub in range(SUBSTEPS):
        rim_field = jnp.concatenate([field[:H], field[blocks - H :]], axis=0)
        outer = padded(rim_field, (("dom", 0),), H)
        extended = jnp.concatenate([outer[:H], field, outer[outer.shape[0] - H :]], axis=0)
        nbrsum = extended[neighbours[:, 0]]
        for slot in range(1, slots):
            nbrsum = nbrsum + extended[neighbours[:, slot]]
        field = advance_rows(field, nbrsum, self_m, edge_m, vert_m)
    level_mask = (jnp.arange(levels, dtype=jnp.int32) == surf_level).astype(jnp.float32)
    return field.at[:, 0].add(level_mask[None, :, None] * received[:, None, :])


def solution(mesh):
    in_specs = (
        P(("grp", "dom"), None, None, None),
        P(("grp", "dom"), None),
        P(("grp", "dom")),
        P(("grp", "dom")),
        P(("grp", "dom")),
        P(("grp", "dom"), None),
        P(),
        P(),
        P(),
    )
    out_specs = P(("grp", "dom"), None, None, None)
    return jax.shard_map(
        per_device, mesh=mesh, in_specs=in_specs, out_specs=out_specs, check_vma=False
    )
```

profile of v0, /device:TPU:1, one launch (start us, length us, event | category | flops | bytes accessed | tf_op | source)
XLA Modules:
  0.0 707.9 jit_solution(6746241704399509085)
XLA Ops:
  6.5 0.0 copy-start
  6.5 0.0 reduce-scatter.2.cloned.1.call-start
  6.5 1.8 fusion.53
  8.4 2.5 collective-permute-start
  10.9 7.0 collective-permute-start.1
  17.9 1.8 slice.67
  19.7 0.7 compare_select_fusion
  20.5 1.0 gather_fusion.8
  21.5 0.7 multiply_add_fusion
  22.2 15.9 %fusion = f32[8192,128]{1,0:T(8,128)} fusion(s32[512]{0:T(512)S(1)} %multiply_add_fusion, f32[512,128]{1,0:T(8,128)} %param.16, f32[512,128]{1,0:T(8,128)S(1)} %gather_fusion.8), kind=kOutput, calls=%fused_computation.10 | convolution fusion | flops 6446710784 | bytes 4720640 | tf_op jit(solution)/shard_map/dot_general | solution.py:55
  38.1 0.0 reduce-scatter.2.cloned.1.call-update
  38.1 0.0 copy-done.5
  38.1 0.0 copy-done
  38.1 0.0 slice-start.4
  38.2 0.0 slice-start.5
  38.2 12.6 %fusion.30 = f32[128,64,4,72]{0,3,2,1:T(8,128)} fusion(f32[64,4,72,128]{3,2,1,0:T(8,128)} %param.11, f32[2,128,128]{2,1,0:T(8,128)S(1)} %copy-done, s32[]{:T(128)S(6)} %select_n.36), kind=kOutput, calls=%fused_computation.40 | convolution fusion | flops 3623878656 | bytes 18939908 | tf_op jit(solution)/shard_map/dot_general | solution.py:28
  50.8 0.0 collective-permute-done
  50.8 0.7 constant_dynamic-update-slice_fusion.2
  51.5 0.0 slice-done.3
  51.5 0.0 slice-done.4
  51.5 0.0 slice-done.5
  51.5 4.2 constant_dynamic-update-slice_fusion.1
  55.8 0.0 collective-permute-done.1
  55.8 0.7 constant_dynamic-update-slice_fusion
  56.5 8.7 %gather_fusion = f32[64,4,72,128]{3,2,1,0:T(8,128)} fusion(f32[68,4,72,128]{3,2,1,0:T(8,128)} %constant_dynamic-update-slice_fusion, s32[1024]{0:T(1024)S(1)} %get-tuple-element.28), kind=kCustom, calls=%fused_computation | custom fusion | bytes 18874624 | tf_op jit(solution)/shard_map/gather | solution.py:64
  65.2 8.7 %gather_fusion.1 = f32[64,4,72,128]{3,2,1,0:T(8,128)} fusion(f32[68,4,72,128]{3,2,1,0:T(8,128)} %constant_dynamic-update-slice_fusion, s32[1024]{0:T(1024)S(1)} %get-tuple-element.27), kind=kCustom, calls=%fused_computation.1 | custom fusion | bytes 18874624 | tf_op jit(solution)/shard_map/gather | solution.py:66
  73.9 8.6 %gather_fusion.2 = f32[64,4,72,128]{3,2,1,0:T(8,128)} fusion(f32[68,4,72,128]{3,2,1,0:T(8,128)} %constant_dynamic-update-slice_fusion, s32[1024]{0:T(1024)S(1)} %get-tuple-element.26), kind=kCustom, calls=%fused_computation.2 | custom fusion | bytes 18874624 | tf_op jit(solution)/shard_map/gather | solution.py:66
  82.5 8.8 %gather_fusion.3 = f32[64,4,72,128]{3,2,1,0:T(8,128)} fusion(f32[68,4,72,128]{3,2,1,0:T(8,128)} %constant_dynamic-update-slice_fusion, s32[1024]{0:T(1024)S(1)} %get-tuple-element.25), kind=kCustom, calls=%fused_computation.3 | custom fusion | bytes 18874624 | tf_op jit(solution)/shard_map/gather | solution.py:66
  91.3 19.1 %fusion.13 = f32[64,4,72,128]{3,2,1,0:T(8,128)} fusion(f32[64,4,72,128]{3,2,1,0:T(8,128)} %gather_fusion.3, f32[64,4,72,128]{3,2,1,0:T(8,128)} %gather_fusion.2, f32[64,4,72,128]{3,2,1,0:T(8,128)} %gather_fusion, f32[64,4,72,128]{3,2,1,0:T(8,128)} %gather_fusion.1, f32[2,128,128]{2,1,0:T(8,128)S(1)} %copy-done.3, s32[]{:T(128)S(6)} %select_n.36), kind=kOutput, calls=%fused_computation.24 | convolution fusion | flops 3630956544 | bytes 47251460 | tf_op jit(solution)/shard_map/dot_general | solution.py:29
  110.4 14.8 %fusion.20 = f32[64,4,72,128]{3,2,1,0:T(8,128)S(1)} fusion(f32[64,4,72,128]{3,2,1,0:T(8,128)} %param.11, f32[64,4,72,128]{3,2,1,0:T(8,128)} %fusion.13, f32[128,64,4,72]{0,3,2,1:T(8,128)} %fusion.30, f32[2,72,72]{2,1,0:T(8,128)S(1)} %copy-done.4, s32[]{:T(128)S(6)} %select_n.36), kind=kOutput, calls=%fused_computation.31 | convolution fusion | flops 2045509632 | bytes 37785604 | tf_op jit(solution)/shard_map/lm,bfmc->bflc/dot_general | solution.py:31
  125.3 0.0 copy-start.2
  125.3 0.1 collective-permute-start.2
  125.4 7.2 %collective-permute-start.3 = (f32[2,4,72,128]{3,2,1,0:T(8,128)S(1)}, f32[2,4,72,128]{3,2,1,0:T(8,128)S(1)}, u32[]{:S(2)}, u32[]{:S(2)}) collective-permute-start(f32[2,4,72,128]{3,2,1,0:T(8,128)S(1)} %get-tuple-element.18), channel_id=1, source_target_pairs={{1,0},{2,1},{3,2},{4,3},{5,4},{6,5},{7,6},{8,7},{9,8},{10,9},{11,1... | collective-permute-start | bytes 884744 | tf_op jit(solution)/shard_map/ppermute | solution.py:19
  132.6 9.9 %fusion.28 = f32[64,4,72,128]{3,2,1,0:T(8,128)} fusion(f32[64,4,72,128]{3,2,1,0:T(8,128)S(1)} %fusion.20, f32[2,128,128]{2,1,0:T(8,128)S(1)} %copy-done, s32[]{:T(128)S(6)} %select_n.36), kind=kOutput, calls=%fused_computation.38 | convolution fusion | flops 3623878656 | bytes 18939908 | tf_op jit(solution)/shard_map/dot_general | solution.py:28
  142.5 0.0 collective-permute-done.2
  142.5 0.0 collective-permute-done.3
  142.5 8.2 %pad_maximum_fusion = f32[68,4,72,128]{3,2,1,0:T(8,128)} fusion(f32[2,4,72,128]{3,2,1,0:T(8,128)S(1)} %collective-permute-done.3, f32[64,4,72,128]{3,2,1,0:T(8,128)} %copy-done.2, f32[2,4,72,128]{3,2,1,0:T(8,128)S(1)} %collective-permute-done.2), kind=kLoop, calls=%fused_computation.11 | loop fusion | flops 5013504 | bytes 20054016 | tf_op jit(solution)/shard_map/concatenate | solution.py:63
  150.7 8.7 %gather_fusion.4 = f32[64,4,72,128]{3,2,1,0:T(8,128)} fusion(f32[68,4,72,128]{3,2,1,0:T(8,128)} %pad_maximum_fusion, s32[1024]{0:T(1024)S(1)} %get-tuple-element.28), kind=kCustom, calls=%fused_computation.4 | custom fusion | bytes 18874624 | tf_op jit(solution)/shard_map/gather | solution.py:64
  159.4 8.5 %gather_fusion.5 = f32[64,4,72,128]{3,2,1,0:T(8,128)} fusion(f32[68,4,72,128]{3,2,1,0:T(8,128)} %pad_maximum_fusion, s32[1024]{0:T(1024)S(1)} %get-tuple-element.27), kind=kCustom, calls=%fused_computation.5 | custom fusion | bytes 18874624 | tf_op jit(solution)/shard_map/gather | solution.py:66
  167.9 8.7 %gather_fusion.6 = f32[64,4,72,128]{3,2,1,0:T(8,128)} fusion(f32[68,4,72,128]{3,2,1,0:T(8,128)} %pad_maximum_fusion, s32[1024]{0:T(1024)S(1)} %get-tuple-element.26), kind=kCustom, calls=%fused_computation.6 | custom fusion | bytes 18874624 | tf_op jit(solution)/shard_map/gather | solution.py:66
  176.6 8.7 %gather_fusion.7 = f32[64,4,72,128]{3,2,1,0:T(8,128)} fusion(f32[68,4,72,128]{3,2,1,0:T(8,128)} %pad_maximum_fusion, s32[1024]{0:T(1024)S(1)} %get-tuple-element.25), kind=kCustom, calls=%fused_computation.7 | custom fusion | bytes 18874624 | tf_op jit(solution)/shard_map/gather | solution.py:66
  185.4 20.1 %fusion.9 = f32[64,4,72,128]{3,2,1,0:T(8,128)} fusion(f32[64,4,72,128]{3,2,1,0:T(8,128)} %gather_fusion.7, f32[64,4,72,128]{3,2,1,0:T(8,128)} %gather_fusion.6, f32[64,4,72,128]{3,2,1,0:T(8,128)} %gather_fusion.4, f32[64,4,72,128]{3,2,1,0:T(8,128)} %gather_fusion.5, f32[2,128,128]{2,1,0:T(8,128)S(1)} %copy-done.3, s32[]{:T(128)S(6)} %select_n.36), kind=kOutput, calls=%fused_computation.20 | convolution fusion | flops 3630956544 | bytes 47251460 | tf_op jit(solution)/shard_map/dot_general | solution.py:29
  205.5 0.0 slice-done
  205.5 15.9 %fusion.5 = f32[64,4,128,72]{2,3,1,0:T(8,128)} fusion(f32[64,4,72,128]{3,2,1,0:T(8,128)S(1)} %bitcast.57, f32[64,4,72,128]{3,2,1,0:T(8,128)} %fusion.28, f32[64,4,72,128]{3,2,1,0:T(8,128)} %fusion.9, f32[2,72,72]{2,1,0:T(8,128)S(1)} %copy-done.4, s32[]{:T(128)S(6)} %select_n.36), kind=kOutput, calls=%fused_computation.16 | convolution fusion | flops 2045509632 | bytes 37785604 | tf_op jit(solution)/shard_map/lm,bfmc->bflc/dot_general | solution.py:31
  221.4 8.1 %copy.15 = f32[64,4,72,128]{3,2,1,0:T(8,128)} copy(f32[64,4,72,128]{3,2,1,0:T(8,128)} %bitcast.61) | data formatting | bytes 18874368
  229.4 468.0 %reduce-scatter.2.cloned.1.call-done = f32[64,128]{1,0:T(8,128)} async-done(((f32[8192,128]{1,0:T(8,128)}), f32[64,128]{1,0:T(8,128)}) %reduce-scatter.2.cloned.1.call-update) | async-done | bytes 32784 | tf_op jit(solution)/shard_map/reduce_scatter | solution.py:58
  697.4 3.4 fusion.24
  700.8 0.0 copy-done.1
  (22 shorter events, 0.1 us)
Async XLA Ops:
  6.5 31.6 %copy-start = (f32[2,128,128]{2,1,0:T(8,128)S(1)}, f32[2,128,128]{2,1,0:T(8,128)}, u32[]{:S(2)}) copy-start(f32[2,128,128]{2,1,0:T(8,128)} %param.17) | copy-start | bytes 393220
  6.5 690.9 %reduce-scatter.2.cloned.1.call-start = ((), (), s32[]{:S(2)}) async-start(), calls=%async_computation.1 | async-start | bytes 4227072 | tf_op jit(solution)/shard_map/reduce_scatter | solution.py:58
  8.4 42.4 %collective-permute-start = (f32[2,4,72,128]{3,2,1,0:T(8,128)}, f32[2,4,72,128]{3,2,1,0:T(8,128)S(1)}, u32[]{:S(2)}, u32[]{:S(2)}) collective-permute-start(f32[2,4,72,128]{3,2,1,0:T(8,128)} %get-tuple-element.20), channel_id=1, source_target_pairs={{0,1},{1,2},{2,3},{3,4},{4,5},{5,6},{6,7},{7,8},{8,9},{9,10},{10,1... | collective-permute-start | bytes 884744 | tf_op jit(solution)/shard_map/ppermute | solution.py:17
  10.9 44.9 %collective-permute-start.1 = (f32[2,4,72,128]{3,2,1,0:T(8,128)S(1)}, f32[2,4,72,128]{3,2,1,0:T(8,128)S(1)}, u32[]{:S(2)}, u32[]{:S(2)}) collective-permute-start(f32[2,4,72,128]{3,2,1,0:T(8,128)S(1)} %get-tuple-element.19), channel_id=1, source_target_pairs={{1,0},{2,1},{3,2},{4,3},{5,4},{6,5},{7,6},{8,7},{9,8},{10,9},{11,1... | collective-permute-start | bytes 884744 | tf_op jit(solution)/shard_map/ppermute | solution.py:19
  17.9 20.2 %copy-start.5 = (s32[64,4]{0,1:T(4,128)S(1)}, s32[64,4]{0,1:T(4,128)}, u32[]{:S(2)}) copy-start(s32[64,4]{0,1:T(4,128)} %param.12) | copy-start | bytes 3076
  38.1 13.4 %slice-start.3 = ((s8[9437184]{0:T(1024)(128)(4,1)}), s8[1048576]{0:T(1024)(128)(4,1)S(1)}, s32[]{:S(2)}) async-start(s8[9437184]{0:T(1024)(128)(4,1)} %bitcast.59), calls=%async_computation.5 | async-start | bytes 2097152
  38.1 13.4 %slice-start.4 = ((s8[9437184]{0:T(1024)(128)(4,1)}), s8[4194304]{0:T(1024)(128)(4,1)S(1)}, s32[]{:S(2)}) async-start(s8[9437184]{0:T(1024)(128)(4,1)} %bitcast.59), calls=%async_computation.6 | async-start | bytes 8388608
  38.2 13.4 %slice-start.5 = ((s8[9437184]{0:T(1024)(128)(4,1)}), s8[4194304]{0:T(1024)(128)(4,1)S(1)}, s32[]{:S(2)}) async-start(s8[9437184]{0:T(1024)(128)(4,1)} %bitcast.59), calls=%async_computation.7 | async-start | bytes 8388608
  82.5 8.8 %copy-start.3 = (f32[2,128,128]{2,1,0:T(8,128)S(1)}, f32[2,128,128]{2,1,0:T(8,128)}, u32[]{:S(2)}) copy-start(f32[2,128,128]{2,1,0:T(8,128)} %param.18) | copy-start | bytes 393220
  91.3 19.1 %copy-start.4 = (f32[2,72,72]{2,1,0:T(8,128)S(1)}, f32[2,72,72]{2,1,0:T(8,128)}, u32[]{:S(2)}) copy-start(f32[2,72,72]{2,1,0:T(8,128)} %param.19) | copy-start | bytes 124420
  125.3 17.3 %copy-start.2 = (f32[64,4,72,128]{3,2,1,0:T(8,128)}, f32[64,4,72,128]{3,2,1,0:T(8,128)S(1)}, u32[]{:S(2)}) copy-start(f32[64,4,72,128]{3,2,1,0:T(8,128)S(1)} %fusion.20) | copy-start | bytes 28311556
  125.3 17.2 %collective-permute-start.2 = (f32[2,4,72,128]{3,2,1,0:T(8,128)S(1)}, f32[2,4,72,128]{3,2,1,0:T(8,128)S(1)}, u32[]{:S(2)}, u32[]{:S(2)}) collective-permute-start(f32[2,4,72,128]{3,2,1,0:T(8,128)S(1)} %get-tuple-element.17), channel_id=1, source_target_pairs={{0,1},{1,2},{2,3},{3,4},{4,5},{5,6},{6,7},{7,8},{8,9},{9,10},{10,1... | collective-permute-start | bytes 884744 | tf_op jit(solution)/shard_map/ppermute | solution.py:17
  125.4 17.1 %collective-permute-start.3 = (f32[2,4,72,128]{3,2,1,0:T(8,128)S(1)}, f32[2,4,72,128]{3,2,1,0:T(8,128)S(1)}, u32[]{:S(2)}, u32[]{:S(2)}) collective-permute-start(f32[2,4,72,128]{3,2,1,0:T(8,128)S(1)} %get-tuple-element.18), channel_id=1, source_target_pairs={{1,0},{2,1},{3,2},{4,3},{5,4},{6,5},{7,6},{8,7},{9,8},{10,9},{11,1... | collective-permute-start | bytes 884744 | tf_op jit(solution)/shard_map/ppermute | solution.py:19
  176.6 28.9 %slice-start = ((s8[9437184]{0:T(1024)(128)(4,1)}), s8[1048576]{0:T(1024)(128)(4,1)S(1)}, s32[]{:S(2)}) async-start(s8[9437184]{0:T(1024)(128)(4,1)} %bitcast.56), calls=%async_computation.2 | async-start | bytes 2097152
  185.3 20.1 %slice-start.1 = ((s8[9437184]{0:T(1024)(128)(4,1)}), s8[4194304]{0:T(1024)(128)(4,1)S(1)}, s32[]{:S(2)}) async-start(s8[9437184]{0:T(1024)(128)(4,1)} %bitcast.56), calls=%async_computation.3 | async-start | bytes 8388608
  185.4 20.1 %slice-start.2 = ((s8[9437184]{0:T(1024)(128)(4,1)}), s8[4194304]{0:T(1024)(128)(4,1)S(1)}, s32[]{:S(2)}) async-start(s8[9437184]{0:T(1024)(128)(4,1)} %bitcast.56), calls=%async_computation.4 | async-start | bytes 8388608
  221.4 479.4 %copy-start.1 = (f32[2,128,128]{2,1,0:T(8,128)S(1)}, f32[2,128,128]{2,1,0:T(8,128)}, u32[]{:S(2)}) copy-start(f32[2,128,128]{2,1,0:T(8,128)} %param.17) | copy-start | bytes 393220
Sparse Core Ops, SparseCore 0:
  38.2 659.1 reduce-scatter.1
where the time goes:
time: 718 us; the launch traced here: 708 us
  waiting for transfers between devices  468 us (65%)
  matrix products  108 us (15%)
  local copies, waits for them, and re-layouts  88 us (12%)
  starting transfers between devices  16.8 us (2%)
  between operations  13.8 us (2%)
  other arithmetic  13 us (2%)
    reduce_scatter x1, waiting for transfers between devices, per_device(): lax.psum_scatter(dense, ('grp', 'dom'), scatter_dimension=0, tiled=True)  468 us
    gather x6, local copies, waits for them, and re-layouts, per_device(): nbrsum = nbrsum + extended[neighbours[:, slot]]  52.1 us
    dot_general x2, matrix products, advance_rows(): jnp.matmul(nbrsum, edge_m, precision=lax.Precision.HIGHEST)  39.2 us
    dot_general x2, matrix products, advance_rows(): jnp.einsum('lm,bfmc->bflc', vert_m, lateral, precision=lax.Precision.HIGH...  30.7 us
    dot_general x2, matrix products, advance_rows(): jnp.matmul(center, self_m, precision=lax.Precision.HIGHEST)  22.5 us
    gather x2, local copies, waits for them, and re-layouts, per_device(): nbrsum = extended[neighbours[:, 0]]  17.3 us
    dot_general x1, matrix products, per_device(): lax.dot_general(select, values, (((0,), (0,)), ((), ())), precision=lax.P...  15.9 us
  transfers between devices with their start and end apart: 5, of which 1 were waited for; matrix products, arithmetic and copies ran while one was open for 29% of the time, Pallas kernels for 0%

commit v1 on v0

v1 whole, which is shorter than its diff:
```python
import functools

import jax
import jax.numpy as jnp
from jax import lax
from jax.experimental import pallas as pl
from jax.experimental.pallas import tpu as pltpu
from jax.sharding import PartitionSpec as P

MESH = pl.DeviceIdType.MESH
F32 = jnp.float32
BF16 = jnp.bfloat16
NZ = 4
CAP = 16
RIM = 4
RELAY = 1
ROWS = NZ * CAP
MSG = ROWS + 8
CHUNKS = 4


def split(v):
    hi = v.astype(BF16)
    return hi, (v - hi.astype(F32)).astype(BF16)


def dot(a, b):
    return jnp.dot(a, b, preferred_element_type=F32)


def dot_nt(a, b):
    return lax.dot_general(a, b, (((1,), (1,)), ((), ())), preferred_element_type=F32)


def exact(a, b):
    return jnp.dot(a, b, precision=lax.Precision.HIGHEST, preferred_element_type=F32)


def pick(onehot, v):
    hi, lo = split(v)
    both = dot(onehot, jnp.concatenate([hi, lo], axis=1))
    width = v.shape[1]
    return both[:, :width] + both[:, width:]


def iota(shape, dim):
    return lax.broadcasted_iota(jnp.int32, shape, dim)


def kernel(
    n_grp, n_dom,
    state, nbr_in, dest_in, src_in, blk_in, wts_in, self_in, edge_in, vert_in,
    out,
    xv, nx, hl, hr, nbr, dest, src, blk, wts, selfv, edgev, vertv,
    wa, wc, vcat, mo, ml, mr, sb, rb, fb, fid, db, ob, gb, tot,
    sem_x, sem_in, sem_halo_s, sem_halo_r, sem_m_s, sem_m_r,
    sem_p1_s, sem_p1_r, sem_p2_s, sem_p2_r, sem_p3_s, sem_p3_r,
):
    blocks, fields, lev, cols = state.shape
    n_gi = n_dom // NZ
    lanes = n_gi * CAP
    ocean_g = n_grp - 1
    g = lax.axis_index("grp")
    d = lax.axis_index("dom")
    gi = d // NZ
    z = lax.rem(d, NZ)
    is_ocean = g == ocean_g
    is_relay = g == RELAY
    comp = jnp.where(is_ocean, 1, 0)
    right = (g, lax.rem(d + 1, n_dom))
    left = (g, lax.rem(d + n_dom - 1, n_dom))

    per = blocks // CHUNKS
    loads_x = [
        pltpu.make_async_copy(
            state.at[pl.ds(i * per, per)], xv.at[pl.ds(i * per, per)], sem_x.at[i]
        )
        for i in range(CHUNKS)
    ]
    pairs = [
        (nbr_in, nbr), (dest_in, dest), (src_in, src), (blk_in, blk), (wts_in, wts),
        (self_in.at[comp], selfv), (edge_in.at[comp], edgev), (vert_in.at[comp], vertv),
    ]
    loads = [pltpu.make_async_copy(a, b, sem_in.at[i]) for i, (a, b) in enumerate(pairs)]
    for c in loads:
        c.start()
    for c in loads_x:
        c.start()

    barrier = pltpu.get_barrier_semaphore()

    def greet(gg, dd):
        pl.semaphore_signal(barrier, inc=1, device_id=(gg, dd), device_id_type=MESH)

    greet(*left)
    greet(*right)

    @pl.when(is_ocean)
    def _():
        for q in range(n_gi):
            for gg in range(ocean_g):
                greet(gg, q * NZ + z)
        for r in range(1, NZ):
            greet(ocean_g, gi * NZ + lax.rem(z + r, NZ))

    @pl.when(jnp.logical_not(is_ocean))
    def _():
        for q in range(n_gi):
            greet(ocean_g, q * NZ + z)

    @pl.when(is_relay)
    def _():
        for r in range(1, NZ):
            greet(RELAY, gi * NZ + lax.rem(z + r, NZ))
        for gg in range(ocean_g):
            if gg != RELAY:
                greet(gg, d)

    @pl.when(jnp.logical_not(jnp.logical_or(is_relay, is_ocean)))
    def _():
        greet(RELAY, d)

    greetings = jnp.where(
        is_ocean,
        2 + n_gi * ocean_g + NZ - 1,
        jnp.where(is_relay, 2 + n_gi + NZ - 1 + ocean_g - 1, 2 + n_gi + 1),
    )
    pl.semaphore_wait(barrier, greetings)

    halo = []
    for f in range(fields):
        halo.append(
            pltpu.make_async_remote_copy(
                src_ref=state.at[pl.ds(blocks - RIM, RIM), f], dst_ref=hl.at[f],
                send_sem=sem_halo_s.at[0, f], recv_sem=sem_halo_r.at[0, f],
                device_id=right, device_id_type=MESH,
            )
        )
        halo.append(
            pltpu.make_async_remote_copy(
                src_ref=state.at[pl.ds(0, RIM), f], dst_ref=hr.at[f],
                send_sem=sem_halo_s.at[1, f], recv_sem=sem_halo_r.at[1, f],
                device_id=left, device_id_type=MESH,
            )
        )
    for c in halo:
        c.start()

    loads[0].wait()
    mo[...] = jnp.zeros_like(mo)
    for side in range(2):
        for k in range(2):
            b = k if side == 0 else blocks - 2 + k
            third = nbr[b, 2]
            fourth = nbr[b, 3]
            for j in range(5):
                count = jnp.where(third == b + j, 1.0, 0.0) + jnp.where(fourth == b + j, 1.0, 0.0)
                row = side * 16 + k * 5 + j
                mo[row : row + 1, :] = jnp.full((1, cols), count, F32)
    counts = [
        pltpu.make_async_remote_copy(
            src_ref=mo.at[pl.ds(16, 16)], dst_ref=ml, send_sem=sem_m_s.at[0],
            recv_sem=sem_m_r.at[0], device_id=right, device_id_type=MESH,
        ),
        pltpu.make_async_remote_copy(
            src_ref=mo.at[pl.ds(0, 16)], dst_ref=mr, send_sem=sem_m_s.at[1],
            recv_sem=sem_m_r.at[1], device_id=left, device_id_type=MESH,
        ),
    ]
    for c in counts:
        c.start()

    for c in loads[1:5]:
        c.wait()
    n_rows = n_dom * CAP
    key = lax.rem(dest[...], n_dom)
    code = blk[...] + jnp.where(is_ocean, blocks, 0) * (dest[...] // n_dom)
    toward = (iota((n_dom, n_rows), 0) == key).astype(BF16)
    before = (iota((n_rows, n_rows), 0) < iota((n_rows, n_rows), 1)).astype(BF16)
    rank = jnp.sum(toward.astype(F32) * dot(toward, before), axis=0, keepdims=True)
    slot = key.astype(F32) * CAP + rank
    perm = (iota((n_rows, n_rows), 0).astype(F32) == slot).astype(BF16)
    weights = pick(perm, wts[...])
    origin = (iota((blocks, n_rows), 0) == src[...]).astype(BF16)
    origin = dot_nt(perm, origin).astype(BF16)
    lane = (gi * CAP).astype(F32) + rank
    at_lane = (iota((cols, n_rows), 0).astype(F32) == lane).astype(BF16)
    key8 = (key // NZ) * 8 + lax.rem(key, NZ)
    coded = jnp.where(iota((n_gi * 8, n_rows), 0) == key8, code.astype(F32), 0.0).astype(BF16)
    targets = dot_nt(coded, at_lane)
    for c in loads_x:
        c.wait()
    surface = jnp.where(is_ocean, xv[:, 0, 0, :], xv[:, 0, lev - 1, :])
    values = weights * pick(origin, surface)
    sb[:, 0:ROWS, :] = values.reshape(n_gi, ROWS, cols)
    sb[:, ROWS:MSG, :] = targets.reshape(n_gi, 8, cols)
    to_grp = jnp.where(is_ocean, RELAY, ocean_g)
    my_slot = jnp.where(is_ocean, gi, g * n_gi + gi)
    first = [
        pltpu.make_async_remote_copy(
            src_ref=sb.at[q], dst_ref=rb.at[my_slot], send_sem=sem_p1_s.at[q],
            recv_sem=sem_p1_r.at[my_slot], device_id=(to_grp, q * NZ + z), device_id_type=MESH,
        )
        for q in range(n_gi)
    ]
    for c in first:
        c.start()

    for c in loads[5:]:
        c.wait()
    eye = (iota((cols, cols), 0) == iota((cols, cols), 1)).astype(F32)
    a = eye + 0.5 * selfv[...]
    e = 0.5 * edgev[...]
    a2h, a2l = split(exact(a, a))
    ch, cl = split(exact(e, a) + exact(a, e))
    e2h, e2l = split(exact(e, e))
    wa[0:cols, 0:cols] = a2h
    wa[0:cols, cols : 2 * cols] = a2l
    wa[cols : 2 * cols, 0:cols] = ch
    wa[cols : 2 * cols, cols : 2 * cols] = cl
    for half in range(2):
        wc[half * cols : (half + 1) * cols, 0:cols] = e2h
        wc[half * cols : (half + 1) * cols, cols : 2 * cols] = e2l
    v2 = exact(vertv[...], vertv[...])
    v2h = v2.astype(BF16).astype(F32)
    vcat[...] = jnp.concatenate([v2h, v2h, v2 - v2h], axis=1).astype(BF16)

    def lateral(x, n1, n2):
        xh, xl = split(x)
        n1h, n1l = split(n1)
        n2h, n2l = split(n2)
        p = dot(jnp.concatenate([xh, n1h], axis=1), wa[...])
        p += dot(jnp.concatenate([xl, n1l], axis=1), wa[...])
        p += dot(jnp.concatenate([n2h, n2l], axis=1), wc[...])
        return p[:, 0:cols] + p[:, cols:]

    def vertical(v):
        hi = v.astype(BF16).astype(F32)
        return dot(vcat[...], jnp.concatenate([hi, v - hi, hi], axis=0).astype(BF16))

    def near(b):
        third_ = jnp.clip(nbr[b, 2] - 2, 0, blocks - 1)
        fourth_ = jnp.clip(nbr[b, 3] - 2, 0, blocks - 1)
        return xv[b - 1] + xv[b + 1] + xv[third_] + xv[fourth_]

    def inner(b, carry):
        x = xv[b].reshape(fields * lev, cols)
        n1 = nx[b + 2].reshape(fields * lev, cols)
        n2 = (nx[b + 1] + nx[b + 3] + nx[nbr[b, 2]] + nx[nbr[b, 3]]).reshape(fields * lev, cols)
        lat = lateral(x, n1, n2)
        for f in range(0, fields, 2):
            pair = jnp.concatenate(
                [lat[f * lev : (f + 1) * lev], lat[(f + 1) * lev : (f + 2) * lev]], axis=1
            )
            res = vertical(pair)
            out[b, f] = res[:, 0:cols]
            out[b, f + 1] = res[:, cols:]
        later = jnp.minimum(b + 3, blocks - 3)
        nx[later + 2] = near(later)
        return carry

    for b in range(2, 7):
        nx[b + 2] = near(b)
    span = blocks - 2 * RIM
    cuts = [RIM, RIM + span // 3, RIM + 2 * span // 3, blocks - RIM]
    lax.fori_loop(cuts[0], cuts[1], inner, 0)

    def received_wait(dst, sem):
        pltpu.make_async_remote_copy(
            src_ref=dst, dst_ref=dst, send_sem=sem, recv_sem=sem,
            device_id=left, device_id_type=MESH,
        ).wait_recv()

    def dense(rows, ids, height):
        return pick((iota((height, lanes), 0) == ids).astype(BF16), rows)

    def second(make):
        return [make(r, gi * NZ + lax.rem(z + r, NZ)) for r in range(1, NZ)]

    def ocean_copy(r, dd):
        return pltpu.make_async_remote_copy(
            src_ref=db.at[lax.rem(z + r, NZ)], dst_ref=ob.at[z], send_sem=sem_p2_s.at[r, 0],
            recv_sem=sem_p2_r.at[z, 0], device_id=(ocean_g, dd), device_id_type=MESH,
        )

    def relay_rows(r, dd):
        zz = lax.rem(z + r, NZ)
        return pltpu.make_async_remote_copy(
            src_ref=rb.at[pl.ds(0, n_gi), pl.ds(pl.multiple_of(zz * CAP, CAP), CAP)],
            dst_ref=fb.at[z], send_sem=sem_p2_s.at[r, 0],
            recv_sem=sem_p2_r.at[z, 0], device_id=(RELAY, dd), device_id_type=MESH,
        )

    def relay_ids(r, dd):
        return pltpu.make_async_remote_copy(
            src_ref=rb.at[pl.ds(0, n_gi), pl.ds(ROWS, 8)],
            dst_ref=fid.at[z], send_sem=sem_p2_s.at[r, 1],
            recv_sem=sem_p2_r.at[z, 1], device_id=(RELAY, dd), device_id_type=MESH,
        )

    @pl.when(is_ocean)
    def _():
        for s in range(ocean_g * n_gi):
            received_wait(rb.at[s], sem_p1_r.at[s])
        for zz in range(NZ):
            total = jnp.zeros((blocks, cols), F32)
            for gg in range(ocean_g):
                sl = slice(gg * n_gi, (gg + 1) * n_gi)
                rows = rb[sl, zz * CAP : (zz + 1) * CAP, :].reshape(lanes, cols)
                ids = jnp.sum(rb[sl, ROWS:MSG, :], axis=0)[zz : zz + 1, 0:lanes].astype(jnp.int32)
                total += dense(rows, ids, blocks)
            db[zz] = total
        for c in second(ocean_copy):
            c.start()

    @pl.when(is_relay)
    def _():
        for s in range(n_gi):
            received_wait(rb.at[s], sem_p1_r.at[s])
        for c in second(relay_rows) + second(relay_ids):
            c.start()

    lax.fori_loop(cuts[1], cuts[2], inner, 0)

    def third(gg, slot_):
        return pltpu.make_async_remote_copy(
            src_ref=tot.at[pl.ds(gg * blocks, blocks)], dst_ref=gb,
            send_sem=sem_p3_s.at[slot_], recv_sem=sem_p3_r.at[0],
            device_id=(gg, d), device_id_type=MESH,
        )

    def thirds():
        others = [gg for gg in range(ocean_g) if gg != RELAY]
        return [third(gg, i) for i, gg in enumerate(others)]

    @pl.when(is_relay)
    def _():
        own_rows = rb[0:n_gi, pl.ds(pl.multiple_of(z * CAP, CAP), CAP), :]
        own_ids = rb[0:n_gi, ROWS:MSG, :]

        def add(rows, ids8):
            mine = jnp.where(iota((8, cols), 0) == z, jnp.sum(ids8, axis=0), 0.0)
            ids = jnp.sum(mine, axis=0, keepdims=True)[:, 0:lanes].astype(jnp.int32)
            return dense(rows.reshape(lanes, cols), ids, ocean_g * blocks)

        tot[...] = add(own_rows, own_ids)
        for r in range(1, NZ):
            zz = lax.rem(z + r, NZ)
            received_wait(fb.at[zz], sem_p2_r.at[zz, 0])
            received_wait(fid.at[zz], sem_p2_r.at[zz, 1])
            tot[...] += add(fb[zz], fid[zz])
        for c in thirds():
            c.start()

    lax.fori_loop(cuts[2], cuts[3], inner, 0)

    for c in counts:
        c.wait_recv()
    for f in range(fields):
        halo[2 * f].wait_recv()
        halo[2 * f + 1].wait_recv()
        for side in range(2):
            base = 0 if side == 0 else blocks - RIM

            def at(k):
                if side == 0:
                    return hl[f, k] if k < RIM else xv[k - RIM, f]
                return xv[blocks - RIM + k, f] if k < RIM else hr[f, k - RIM]

            for k in range(2, 6):
                outer = k < 4 if side == 0 else k >= 4
                if side == 0:
                    m, row = (ml, (k - 2) * 5) if outer else (mo, (k - 4) * 5)
                else:
                    m, row = (mr, (k - 4) * 5) if outer else (mo, 16 + (k - 2) * 5)
                acc = at(k - 1) + at(k + 1)
                for j in range(5):
                    acc += m[row + j : row + j + 1, :] * at(k - 2 + j)
                at_row = k - 2 if side == 0 else blocks - 2 + k
                nx[at_row, f] = acc
            xs, n1s, n2s = [], [], []
            for k in range(RIM):
                b = base + k
                xs.append(xv[b, f])
                n1s.append(nx[b + 2, f])
                n2s.append(nx[b + 1, f] + nx[b + 3, f] + nx[nbr[b, 2], f] + nx[nbr[b, 3], f])
            lat = lateral(*(jnp.concatenate(v, axis=0) for v in (xs, n1s, n2s)))
            for k in range(0, RIM, 2):
                pair = jnp.concatenate(
                    [lat[k * lev : (k + 1) * lev], lat[(k + 1) * lev : (k + 2) * lev]], axis=1
                )
                res = vertical(pair)
                out[base + k, f] = res[:, 0:cols]
                out[base + k + 1, f] = res[:, cols:]

    @pl.when(is_ocean)
    def _():
        got = db[z]
        for r in range(1, NZ):
            zz = lax.rem(z + r, NZ)
            received_wait(ob.at[zz], sem_p2_r.at[zz, 0])
            got += ob[zz]
        out[:, 0, 0, :] += got
        for c in second(ocean_copy):
            c.wait_send()

    @pl.when(is_relay)
    def _():
        out[:, 0, lev - 1, :] += tot[RELAY * blocks : (RELAY + 1) * blocks, :]
        for c in second(relay_rows) + second(relay_ids) + thirds():
            c.wait_send()

    @pl.when(jnp.logical_not(jnp.logical_or(is_relay, is_ocean)))
    def _():
        received_wait(gb, sem_p3_r.at[0])
        out[:, 0, lev - 1, :] += gb[...]

    for c in halo + counts + first:
        c.wait_send()


def per_device(
    state, neighbours, remap_dest, remap_src, remap_block, remap_weights, self_op, edge_op, vert_op
):
    n_grp = lax.axis_size("grp")
    n_dom = lax.axis_size("dom")
    blocks, fields, lev, cols = state.shape
    n_rows = remap_dest.shape[0]
    n_gi = n_dom // NZ
    dma = pltpu.SemaphoreType.DMA
    vm = pltpu.VMEM
    call = pl.pallas_call(
        functools.partial(kernel, n_grp, n_dom),
        out_shape=pltpu.VMEM(state.shape, F32),
        in_specs=[pl.BlockSpec(memory_space=pl.ANY)] * 9,
        out_specs=pl.BlockSpec(memory_space=pltpu.VMEM),
        scratch_shapes=[
            vm(state.shape, F32),
            vm((blocks + 4, fields, lev, cols), F32),
            vm((fields, RIM, lev, cols), F32),
            vm((fields, RIM, lev, cols), F32),
            pltpu.SMEM(neighbours.shape, jnp.int32),
            vm((1, n_rows), jnp.int32),
            vm((1, n_rows), jnp.int32),
            vm((1, n_rows), jnp.int32),
            vm((n_rows, cols), F32),
            vm((cols, cols), F32),
            vm((cols, cols), F32),
            vm((lev, lev), F32),
            vm((2 * cols, 2 * cols), BF16),
            vm((2 * cols, 2 * cols), BF16),
            vm((lev, 3 * lev), BF16),
            vm((32, cols), F32),
            vm((16, cols), F32),
            vm((16, cols), F32),
            vm((n_gi, MSG, cols), F32),
            vm(((n_grp - 1) * n_gi, MSG, cols), F32),
            vm((NZ, n_gi, CAP, cols), F32),
            vm((NZ, n_gi, 8, cols), F32),
            vm((NZ, blocks, cols), F32),
            vm((NZ, blocks, cols), F32),
            vm((blocks, cols), F32),
            vm(((n_grp - 1) * blocks, cols), F32),
            dma((CHUNKS,)),
            dma((8,)),
            dma((2, fields)),
            dma((2, fields)),
            dma((2,)),
            dma((2,)),
            dma((n_gi,)),
            dma(((n_grp - 1) * n_gi,)),
            dma((NZ, 2)),
            dma((NZ, 2)),
            dma((n_grp - 2,)),
            dma((1,)),
        ],
        compiler_params=pltpu.CompilerParams(
            collective_id=0, has_side_effects=True, vmem_limit_bytes=46 * 1024 * 1024
        ),
        name="interval",
    )
    return call(
        state,
        neighbours,
        remap_dest.reshape(1, n_rows),
        remap_src.reshape(1, n_rows),
        remap_block.reshape(1, n_rows),
        remap_weights,
        self_op,
        edge_op,
        vert_op,
    )


def solution(mesh):
    in_specs = (
        P(("grp", "dom"), None, None, None),
        P(("grp", "dom"), None),
        P(("grp", "dom")),
        P(("grp", "dom")),
        P(("grp", "dom")),
        P(("grp", "dom"), None),
        P(),
        P(),
        P(),
    )
    out_specs = P(("grp", "dom"), None, None, None)
    return jax.shard_map(
        per_device, mesh=mesh, in_specs=in_specs, out_specs=out_specs, check_vma=False
    )
```

time: 718 us -> 56.5 us (0.08)
  the two profiles are of different devices: /device:TPU:1 before, /device:TPU:31 now
where the time goes in v1:
time: 56.5 us; the launch traced here: 56.4 us
  Pallas kernels  51.3 us (91%)
  local copies, waits for them, and re-layouts  5.13 us (9%)
    pallas_call x1, Pallas kernels, per_device(): call(state, neighbours, remap_dest.reshape(1, n_rows), remap_src.reshape(...  51.3 us
    unnamed x2, local copies, waits for them, and re-layouts  5.13 us

profile of v1, /device:TPU:31, one launch (start us, length us, event | category | flops | bytes accessed | tf_op | source)
XLA Modules:
  0.0 56.4 jit_solution(4598778927950750771)
XLA Ops:
  0.0 1.4 %copy.10.nbr_in = s32[64,4]{1,0:T(8,128)} copy(s32[64,4]{0,1:T(4,128)} %param.10) | data formatting | bytes 2048 | tf_op args[1]
  1.4 51.3 %interval.1 = f32[64,4,72,128]{3,2,1,0:T(8,128)S(1)} custom-call(f32[64,4,72,128]{3,2,1,0:T(8,128)} %state.1, s32[64,4]{1,0:T(8,128)} %copy.10.nbr_in, s32[1,512]{1,0:T(1,128)} %bitcast.3, s32[1,512]{1,0:T(1,128)} %bitcast.4, s32[1,512]{1,0:T(1,128)} %bitcast.5, f32[512,128]{1,0:T(8,128)} %wts_in.1, f32[2,128,128]{2,1,0:T(8,128)} %self_in.1, ...), custom_call_target="tpu_custom_call" | custom-call | tf_op jit(solution)/shard_map/interval/pallas_call | solution.py:482
  52.7 3.7 %copy.12 = f32[64,4,72,128]{3,2,1,0:T(8,128)} copy(f32[64,4,72,128]{3,2,1,0:T(8,128)S(1)} %interval.1) | data formatting | bytes 18874368

commit v2 on v1

--- a/solution.py
+++ b/solution.py
@@ -17,6 +17,8 @@
 ROWS = NZ * CAP
 MSG = ROWS + 8
 CHUNKS = 4
+UNIT = 8
+SECOND, THIRD = 5, 7
 
 
 def split(v):
@@ -125,8 +127,6 @@
         2 + n_gi * ocean_g + NZ - 1,
         jnp.where(is_relay, 2 + n_gi + NZ - 1 + ocean_g - 1, 2 + n_gi + 1),
     )
-    pl.semaphore_wait(barrier, greetings)
-
     halo = []
     for f in range(fields):
         halo.append(
@@ -143,16 +143,13 @@
                 device_id=left, device_id_type=MESH,
             )
         )
-    for c in halo:
-        c.start()
-
     loads[0].wait()
     mo[...] = jnp.zeros_like(mo)
     for side in range(2):
         for k in range(2):
             b = k if side == 0 else blocks - 2 + k
-            third = nbr[b, 2]
-            fourth = nbr[b, 3]
+            third = nbr[2, b]
+            fourth = nbr[3, b]
             for j in range(5):
                 count = jnp.where(third == b + j, 1.0, 0.0) + jnp.where(fourth == b + j, 1.0, 0.0)
                 row = side * 16 + k * 5 + j
@@ -167,9 +164,6 @@
             recv_sem=sem_m_r.at[1], device_id=left, device_id_type=MESH,
         ),
     ]
-    for c in counts:
-        c.start()
-
     for c in loads[1:5]:
         c.wait()
     n_rows = n_dom * CAP
@@ -203,9 +197,6 @@
         )
         for q in range(n_gi)
     ]
-    for c in first:
-        c.start()
-
     for c in loads[5:]:
         c.wait()
     eye = (iota((cols, cols), 0) == iota((cols, cols), 1)).astype(F32)
@@ -239,31 +230,16 @@
         return dot(vcat[...], jnp.concatenate([hi, v - hi, hi], axis=0).astype(BF16))
 
     def near(b):
-        third_ = jnp.clip(nbr[b, 2] - 2, 0, blocks - 1)
-        fourth_ = jnp.clip(nbr[b, 3] - 2, 0, blocks - 1)
+        third_ = jnp.clip(nbr[2, b] - 2, 0, blocks - 1)
+        fourth_ = jnp.clip(nbr[3, b] - 2, 0, blocks - 1)
         return xv[b - 1] + xv[b + 1] + xv[third_] + xv[fourth_]
 
-    def inner(b, carry):
-        x = xv[b].reshape(fields * lev, cols)
-        n1 = nx[b + 2].reshape(fields * lev, cols)
-        n2 = (nx[b + 1] + nx[b + 3] + nx[nbr[b, 2]] + nx[nbr[b, 3]]).reshape(fields * lev, cols)
-        lat = lateral(x, n1, n2)
-        for f in range(0, fields, 2):
-            pair = jnp.concatenate(
-                [lat[f * lev : (f + 1) * lev], lat[(f + 1) * lev : (f + 2) * lev]], axis=1
-            )
-            res = vertical(pair)
-            out[b, f] = res[:, 0:cols]
-            out[b, f + 1] = res[:, cols:]
-        later = jnp.minimum(b + 3, blocks - 3)
-        nx[later + 2] = near(later)
-        return carry
-
-    for b in range(2, 7):
+    for b in range(2, RIM + UNIT + 2):
         nx[b + 2] = near(b)
-    span = blocks - 2 * RIM
-    cuts = [RIM, RIM + span // 3, RIM + 2 * span // 3, blocks - RIM]
-    lax.fori_loop(cuts[0], cuts[1], inner, 0)
+
+    pl.semaphore_wait(barrier, greetings)
+    for c in halo + counts + first:
+        c.start()
 
     def received_wait(dst, sem):
         pltpu.make_async_remote_copy(
@@ -298,8 +274,7 @@
             recv_sem=sem_p2_r.at[z, 1], device_id=(RELAY, dd), device_id_type=MESH,
         )
 
-    @pl.when(is_ocean)
-    def _():
+    def ocean_second():
         for s in range(ocean_g * n_gi):
             received_wait(rb.at[s], sem_p1_r.at[s])
         for zz in range(NZ):
@@ -313,14 +288,11 @@
         for c in second(ocean_copy):
             c.start()
 
-    @pl.when(is_relay)
-    def _():
+    def relay_second():
         for s in range(n_gi):
             received_wait(rb.at[s], sem_p1_r.at[s])
         for c in second(relay_rows) + second(relay_ids):
             c.start()
-
-    lax.fori_loop(cuts[1], cuts[2], inner, 0)
 
     def third(gg, slot_):
         return pltpu.make_async_remote_copy(
@@ -333,8 +305,7 @@
         others = [gg for gg in range(ocean_g) if gg != RELAY]
         return [third(gg, i) for i, gg in enumerate(others)]
 
-    @pl.when(is_relay)
-    def _():
+    def relay_third():
         own_rows = rb[0:n_gi, pl.ds(pl.multiple_of(z * CAP, CAP), CAP), :]
         own_ids = rb[0:n_gi, ROWS:MSG, :]
 
@@ -352,46 +323,54 @@
         for c in thirds():
             c.start()
 
-    lax.fori_loop(cuts[2], cuts[3], inner, 0)
-
-    for c in counts:
-        c.wait_recv()
-    for f in range(fields):
-        halo[2 * f].wait_recv()
-        halo[2 * f + 1].wait_recv()
+    def outer_sums():
+        for c in counts + halo:
+            c.wait_recv()
         for side in range(2):
-            base = 0 if side == 0 else blocks - RIM
 
             def at(k):
                 if side == 0:
-                    return hl[f, k] if k < RIM else xv[k - RIM, f]
-                return xv[blocks - RIM + k, f] if k < RIM else hr[f, k - RIM]
+                    return hl[:, k] if k < RIM else xv[k - RIM]
+                return xv[blocks - RIM + k] if k < RIM else hr[:, k - RIM]
 
             for k in range(2, 6):
-                outer = k < 4 if side == 0 else k >= 4
                 if side == 0:
-                    m, row = (ml, (k - 2) * 5) if outer else (mo, (k - 4) * 5)
+                    m, row = (ml, (k - 2) * 5) if k < 4 else (mo, (k - 4) * 5)
                 else:
-                    m, row = (mr, (k - 4) * 5) if outer else (mo, 16 + (k - 2) * 5)
+                    m, row = (mr, (k - 4) * 5) if k >= 4 else (mo, 16 + (k - 2) * 5)
                 acc = at(k - 1) + at(k + 1)
                 for j in range(5):
                     acc += m[row + j : row + j + 1, :] * at(k - 2 + j)
-                at_row = k - 2 if side == 0 else blocks - 2 + k
-                nx[at_row, f] = acc
-            xs, n1s, n2s = [], [], []
-            for k in range(RIM):
-                b = base + k
-                xs.append(xv[b, f])
-                n1s.append(nx[b + 2, f])
-                n2s.append(nx[b + 1, f] + nx[b + 3, f] + nx[nbr[b, 2], f] + nx[nbr[b, 3], f])
-            lat = lateral(*(jnp.concatenate(v, axis=0) for v in (xs, n1s, n2s)))
-            for k in range(0, RIM, 2):
-                pair = jnp.concatenate(
-                    [lat[k * lev : (k + 1) * lev], lat[(k + 1) * lev : (k + 2) * lev]], axis=1
-                )
+                nx[k - 2 if side == 0 else blocks - 2 + k] = acc
+
+    def step(i, carry):
+        pl.when(jnp.logical_and(is_ocean, i == SECOND))(ocean_second)
+        pl.when(jnp.logical_and(is_relay, i == SECOND))(relay_second)
+        pl.when(jnp.logical_and(is_relay, i == THIRD))(relay_third)
+        pl.when(i == steps - 1)(outer_sums)
+        mine = [lax.rem(RIM + i * UNIT + u, blocks) for u in range(UNIT)]
+        high = fields * lev
+        xs = [xv[b].reshape(high, cols) for b in mine]
+        n1s = [nx[b + 2].reshape(high, cols) for b in mine]
+        n2s = [
+            (nx[b + 1] + nx[b + 3] + nx[nbr[2, b]] + nx[nbr[3, b]]).reshape(high, cols)
+            for b in mine
+        ]
+        lat = lateral(*(jnp.concatenate(v, axis=0) for v in (xs, n1s, n2s)))
+        for u, b in enumerate(mine):
+            for f in range(0, fields, 2):
+                o = u * high + f * lev
+                pair = jnp.concatenate([lat[o : o + lev], lat[o + lev : o + 2 * lev]], axis=1)
                 res = vertical(pair)
-                out[base + k, f] = res[:, 0:cols]
-                out[base + k + 1, f] = res[:, cols:]
+                out[b, f] = res[:, 0:cols]
+                out[b, f + 1] = res[:, cols:]
+        for u in range(UNIT):
+            later = jnp.minimum(RIM + (i + 1) * UNIT + 2 + u, blocks - 3)
+            nx[later + 2] = near(later)
+        return carry
+
+    steps = blocks // UNIT
+    lax.fori_loop(0, steps, step, 0)
 
     @pl.when(is_ocean)
     def _():
@@ -439,7 +418,7 @@
             vm((blocks + 4, fields, lev, cols), F32),
             vm((fields, RIM, lev, cols), F32),
             vm((fields, RIM, lev, cols), F32),
-            pltpu.SMEM(neighbours.shape, jnp.int32),
+            pltpu.SMEM(neighbours.shape[::-1], jnp.int32),
             vm((1, n_rows), jnp.int32),
             vm((1, n_rows), jnp.int32),
             vm((1, n_rows), jnp.int32),
@@ -481,7 +460,7 @@
     )
     return call(
         state,
-        neighbours,
+        neighbours.T,
         remap_dest.reshape(1, n_rows),
         remap_src.reshape(1, n_rows),
         remap_block.reshape(1, n_rows),

time: 56.5 us -> 38.3 us (0.68)
  the two profiles are of different devices: /device:TPU:31 before, /device:TPU:1 now
where the time goes in v2:
time: 38.3 us; the launch traced here: 38.2 us
  Pallas kernels  34.4 us (90%)
  local copies, waits for them, and re-layouts  3.74 us (10%)
    pallas_call x1, Pallas kernels, per_device(): call(state, neighbours.T, remap_dest.reshape(1, n_rows), remap_src.reshap...  34.4 us
    unnamed x1, local copies, waits for them, and re-layouts  3.74 us

profile of v2, /device:TPU:1, one launch (start us, length us, event | category | flops | bytes accessed | tf_op | source)
XLA Modules:
  0.0 38.2 jit_solution(14702267899439714203)
XLA Ops:
  0.0 34.4 %interval.1 = f32[64,4,72,128]{3,2,1,0:T(8,128)S(1)} custom-call(f32[64,4,72,128]{3,2,1,0:T(8,128)} %state.1, s32[4,64]{1,0:T(4,128)} %bitcast.4, s32[1,512]{1,0:T(1,128)} %bitcast.5, s32[1,512]{1,0:T(1,128)} %bitcast.6, s32[1,512]{1,0:T(1,128)} %bitcast.7, f32[512,128]{1,0:T(8,128)} %wts_in.1, f32[2,128,128]{2,1,0:T(8,128)} %self_in.1, ...), custom_call_target="tpu_custom_call" | custom-call | tf_op jit(solution)/shard_map/interval/pallas_call | solution.py:461
  34.4 3.7 %copy.11 = f32[64,4,72,128]{3,2,1,0:T(8,128)} copy(f32[64,4,72,128]{3,2,1,0:T(8,128)S(1)} %interval.1) | data formatting | bytes 18874368

commit v3 on v2

--- a/solution.py
+++ b/solution.py
@@ -18,7 +18,8 @@
 MSG = ROWS + 8
 CHUNKS = 4
 UNIT = 8
-SECOND, THIRD = 5, 7
+SECOND = 6
+EARLY = 6
 
 
 def split(v):
@@ -53,7 +54,7 @@
     n_grp, n_dom,
     state, nbr_in, dest_in, src_in, blk_in, wts_in, self_in, edge_in, vert_in,
     out,
-    xv, nx, hl, hr, nbr, dest, src, blk, wts, selfv, edgev, vertv,
+    xv, nx, hl, hr, nbr, dest, src, blk, wts, surf, selfv, edgev, vertv,
     wa, wc, vcat, mo, ml, mr, sb, rb, fb, fid, db, ob, gb, tot,
     sem_x, sem_in, sem_halo_s, sem_halo_r, sem_m_s, sem_m_r,
     sem_p1_s, sem_p1_r, sem_p2_s, sem_p2_r, sem_p3_s, sem_p3_r,
@@ -79,8 +80,10 @@
         )
         for i in range(CHUNKS)
     ]
+    top = pl.multiple_of(jnp.where(is_ocean, 0, lev - 8), 8)
     pairs = [
         (nbr_in, nbr), (dest_in, dest), (src_in, src), (blk_in, blk), (wts_in, wts),
+        (state.at[:, 0, pl.ds(top, 8), :], surf),
         (self_in.at[comp], selfv), (edge_in.at[comp], edgev), (vert_in.at[comp], vertv),
     ]
     loads = [pltpu.make_async_copy(a, b, sem_in.at[i]) for i, (a, b) in enumerate(pairs)]
@@ -164,7 +167,7 @@
             recv_sem=sem_m_r.at[1], device_id=left, device_id_type=MESH,
         ),
     ]
-    for c in loads[1:5]:
+    for c in loads[1:6]:
         c.wait()
     n_rows = n_dom * CAP
     key = lax.rem(dest[...], n_dom)
@@ -182,9 +185,7 @@
     key8 = (key // NZ) * 8 + lax.rem(key, NZ)
     coded = jnp.where(iota((n_gi * 8, n_rows), 0) == key8, code.astype(F32), 0.0).astype(BF16)
     targets = dot_nt(coded, at_lane)
-    for c in loads_x:
-        c.wait()
-    surface = jnp.where(is_ocean, xv[:, 0, 0, :], xv[:, 0, lev - 1, :])
+    surface = jnp.where(is_ocean, surf[:, 0, :], surf[:, 7, :])
     values = weights * pick(origin, surface)
     sb[:, 0:ROWS, :] = values.reshape(n_gi, ROWS, cols)
     sb[:, ROWS:MSG, :] = targets.reshape(n_gi, 8, cols)
@@ -197,7 +198,11 @@
         )
         for q in range(n_gi)
     ]
-    for c in loads[5:]:
+    pl.semaphore_wait(barrier, greetings)
+    for c in first + counts + halo:
+        c.start()
+
+    for c in loads[6:]:
         c.wait()
     eye = (iota((cols, cols), 0) == iota((cols, cols), 1)).astype(F32)
     a = eye + 0.5 * selfv[...]
@@ -234,12 +239,10 @@
         fourth_ = jnp.clip(nbr[3, b] - 2, 0, blocks - 1)
         return xv[b - 1] + xv[b + 1] + xv[third_] + xv[fourth_]
 
+    for c in loads_x:
+        c.wait()
     for b in range(2, RIM + UNIT + 2):
         nx[b + 2] = near(b)
-
-    pl.semaphore_wait(barrier, greetings)
-    for c in halo + counts + first:
-        c.start()
 
     def received_wait(dst, sem):
         pltpu.make_async_remote_copy(
@@ -323,15 +326,28 @@
         for c in thirds():
             c.start()
 
-    def outer_sums():
-        for c in counts + halo:
+    def advance(xs, n1s, n2s):
+        lat = lateral(*(jnp.concatenate(v, axis=0) for v in (xs, n1s, n2s)))
+        res = []
+        for o in range(0, lat.shape[0], 2 * lev):
+            pair = jnp.concatenate([lat[o : o + lev], lat[o + lev : o + 2 * lev]], axis=1)
+            both = vertical(pair)
+            res += [both[:, 0:cols], both[:, cols:]]
+        return res
+
+    def second_sum(b, f=slice(None)):
+        return nx[b + 1, f] + nx[b + 3, f] + nx[nbr[2, b], f] + nx[nbr[3, b], f]
+
+    def outer(f0):
+        two = slice(f0, f0 + 2)
+        for c in (counts if f0 == 0 else []) + halo[2 * f0 : 2 * f0 + 4]:
             c.wait_recv()
         for side in range(2):
 
             def at(k):
                 if side == 0:
-                    return hl[:, k] if k < RIM else xv[k - RIM]
-                return xv[blocks - RIM + k] if k < RIM else hr[:, k - RIM]
+                    return hl[two, k] if k < RIM else xv[k - RIM, two]
+                return xv[blocks - RIM + k, two] if k < RIM else hr[two, k - RIM]
 
             for k in range(2, 6):
                 if side == 0:
@@ -341,36 +357,40 @@
                 acc = at(k - 1) + at(k + 1)
                 for j in range(5):
                     acc += m[row + j : row + j + 1, :] * at(k - 2 + j)
-                nx[k - 2 if side == 0 else blocks - 2 + k] = acc
+                nx[k - 2 if side == 0 else blocks - 2 + k, two] = acc
+        mine = [*range(RIM), *range(blocks - RIM, blocks)]
+        high = 2 * lev
+        res = advance(
+            [xv[b, two].reshape(high, cols) for b in mine],
+            [nx[b + 2, two].reshape(high, cols) for b in mine],
+            [second_sum(b, two).reshape(high, cols) for b in mine],
+        )
+        for u, b in enumerate(mine):
+            out[b, f0] = res[2 * u]
+            out[b, f0 + 1] = res[2 * u + 1]
 
     def step(i, carry):
         pl.when(jnp.logical_and(is_ocean, i == SECOND))(ocean_second)
         pl.when(jnp.logical_and(is_relay, i == SECOND))(relay_second)
-        pl.when(jnp.logical_and(is_relay, i == THIRD))(relay_third)
-        pl.when(i == steps - 1)(outer_sums)
-        mine = [lax.rem(RIM + i * UNIT + u, blocks) for u in range(UNIT)]
+        pl.when(i == EARLY)(lambda: outer(0))
+        mine = [RIM + i * UNIT + u for u in range(UNIT)]
         high = fields * lev
-        xs = [xv[b].reshape(high, cols) for b in mine]
-        n1s = [nx[b + 2].reshape(high, cols) for b in mine]
-        n2s = [
-            (nx[b + 1] + nx[b + 3] + nx[nbr[2, b]] + nx[nbr[3, b]]).reshape(high, cols)
-            for b in mine
-        ]
-        lat = lateral(*(jnp.concatenate(v, axis=0) for v in (xs, n1s, n2s)))
+        res = advance(
+            [xv[b].reshape(high, cols) for b in mine],
+            [nx[b + 2].reshape(high, cols) for b in mine],
+            [second_sum(b).reshape(high, cols) for b in mine],
+        )
         for u, b in enumerate(mine):
-            for f in range(0, fields, 2):
-                o = u * high + f * lev
-                pair = jnp.concatenate([lat[o : o + lev], lat[o + lev : o + 2 * lev]], axis=1)
-                res = vertical(pair)
-                out[b, f] = res[:, 0:cols]
-                out[b, f + 1] = res[:, cols:]
+            for f in range(fields):
+                out[b, f] = res[u * fields + f]
         for u in range(UNIT):
             later = jnp.minimum(RIM + (i + 1) * UNIT + 2 + u, blocks - 3)
             nx[later + 2] = near(later)
         return carry
 
-    steps = blocks // UNIT
-    lax.fori_loop(0, steps, step, 0)
+    lax.fori_loop(0, (blocks - 2 * RIM) // UNIT, step, 0)
+    outer(2)
+    pl.when(is_relay)(relay_third)
 
     @pl.when(is_ocean)
     def _():
@@ -423,6 +443,7 @@
             vm((1, n_rows), jnp.int32),
             vm((1, n_rows), jnp.int32),
             vm((n_rows, cols), F32),
+            vm((blocks, 8, cols), F32),
             vm((cols, cols), F32),
             vm((cols, cols), F32),
             vm((lev, lev), F32),
@@ -441,7 +462,7 @@
             vm((blocks, cols), F32),
             vm(((n_grp - 1) * blocks, cols), F32),
             dma((CHUNKS,)),
-            dma((8,)),
+            dma((9,)),
             dma((2, fields)),
             dma((2, fields)),
             dma((2,)),

time: 38.3 us -> 36.3 us (0.948)
  Pallas kernels: 34.4 us -> 32.4 us
    pallas_call x1, Pallas kernels: 34.4 us -> 32.4 us  [per_device(): call(state, neighbours.T, remap_dest.reshape(1, n_rows), remap_src.reshap...]
where the time goes in v3:
time: 36.3 us; the launch traced here: 36.2 us
  Pallas kernels  32.4 us (89%)
  local copies, waits for them, and re-layouts  3.74 us (10%)
    pallas_call x1, Pallas kernels, per_device(): call(state, neighbours.T, remap_dest.reshape(1, n_rows), remap_src.reshap...  32.4 us
    unnamed x1, local copies, waits for them, and re-layouts  3.74 us

profile of v3, /device:TPU:1, one launch (start us, length us, event | category | flops | bytes accessed | tf_op | source)
XLA Modules:
  0.0 36.2 jit_solution(8012151946352566040)
XLA Ops:
  0.0 32.4 %interval.1 = f32[64,4,72,128]{3,2,1,0:T(8,128)S(1)} custom-call(f32[64,4,72,128]{3,2,1,0:T(8,128)} %state.1, s32[4,64]{1,0:T(4,128)} %bitcast.4, s32[1,512]{1,0:T(1,128)} %bitcast.5, s32[1,512]{1,0:T(1,128)} %bitcast.6, s32[1,512]{1,0:T(1,128)} %bitcast.7, f32[512,128]{1,0:T(8,128)} %wts_in.1, f32[2,128,128]{2,1,0:T(8,128)} %self_in.1, ...), custom_call_target="tpu_custom_call" | custom-call | tf_op jit(solution)/shard_map/interval/pallas_call | solution.py:482
  32.4 3.7 %copy.11 = f32[64,4,72,128]{3,2,1,0:T(8,128)} copy(f32[64,4,72,128]{3,2,1,0:T(8,128)S(1)} %interval.1) | data formatting | bytes 18874368

commit v4 on v3

--- a/solution.py
+++ b/solution.py
@@ -13,6 +13,7 @@
 NZ = 4
 CAP = 16
 RIM = 4
+NEAR = 0
 RELAY = 1
 ROWS = NZ * CAP
 MSG = ROWS + 8
@@ -69,6 +70,20 @@
     z = lax.rem(d, NZ)
     is_ocean = g == ocean_g
     is_relay = g == RELAY
+    is_near = g == NEAR
+    n_y = n_gi // 2
+    y, x_hi = gi // 2, lax.rem(gi, 2)
+    x_lo = g // 2
+    def collector(q):
+        same = lax.rem(q, 2) == x_hi
+        return jnp.where(jnp.where(same, x_lo, 1 - x_lo) == 0, NEAR, ocean_g)
+
+    def senders():
+        res = []
+        for gg in range(ocean_g):
+            hi = jnp.where(x_lo == gg // 2, x_hi, 1 - x_hi)
+            res += [(gg, (yy * 2 + hi) * NZ + z) for yy in range(n_y)]
+        return res
     comp = jnp.where(is_ocean, 1, 0)
     right = (g, lax.rem(d + 1, n_dom))
     left = (g, lax.rem(d + n_dom - 1, n_dom))
@@ -100,21 +115,40 @@
     greet(*left)
     greet(*right)
 
+    def greet_senders(own):
+        for gg, dd in senders():
+            if own and gg == NEAR:
+                pl.when(dd != d)(functools.partial(greet, gg, dd))
+            else:
+                greet(gg, dd)
+
     @pl.when(is_ocean)
     def _():
+        greet_senders(False)
         for q in range(n_gi):
-            for gg in range(ocean_g):
-                greet(gg, q * NZ + z)
+            greet(RELAY, q * NZ + z)
         for r in range(1, NZ):
             greet(ocean_g, gi * NZ + lax.rem(z + r, NZ))
+        for r in range(NZ):
+            greet(NEAR, gi * NZ + r)
 
     @pl.when(jnp.logical_not(is_ocean))
+    def _():
+        for q in range(n_gi):
+            pl.when(jnp.logical_not(jnp.logical_and(is_near, gi == q)))(
+                functools.partial(greet, collector(q), q * NZ + z)
+            )
+
+    @pl.when(is_near)
+    def _():
+        greet_senders(True)
+        for r in range(NZ):
+            greet(ocean_g, gi * NZ + r)
+
+    @pl.when(is_relay)
     def _():
         for q in range(n_gi):
             greet(ocean_g, q * NZ + z)
-
-    @pl.when(is_relay)
-    def _():
         for r in range(1, NZ):
             greet(RELAY, gi * NZ + lax.rem(z + r, NZ))
         for gg in range(ocean_g):
@@ -125,11 +159,13 @@
     def _():
         greet(RELAY, d)
 
-    greetings = jnp.where(
+    n_in = ocean_g * n_y
+    greetings = 2 + n_gi + jnp.where(
         is_ocean,
-        2 + n_gi * ocean_g + NZ - 1,
-        jnp.where(is_relay, 2 + n_gi + NZ - 1 + ocean_g - 1, 2 + n_gi + 1),
+        n_in + NZ - 1 + NZ,
+        jnp.where(is_relay, n_gi + NZ - 1 + ocean_g - 1, jnp.where(is_near, n_in - 2 + NZ + 1, 1)),
     )
+
     halo = []
     for f in range(fields):
         halo.append(
@@ -180,7 +216,8 @@
     weights = pick(perm, wts[...])
     origin = (iota((blocks, n_rows), 0) == src[...]).astype(BF16)
     origin = dot_nt(perm, origin).astype(BF16)
-    lane = (gi * CAP).astype(F32) + rank
+    my_slot = jnp.where(is_ocean, gi, g * n_y + y)
+    lane = (lax.rem(my_slot, n_gi) * CAP).astype(F32) + rank
     at_lane = (iota((cols, n_rows), 0).astype(F32) == lane).astype(BF16)
     key8 = (key // NZ) * 8 + lax.rem(key, NZ)
     coded = jnp.where(iota((n_gi * 8, n_rows), 0) == key8, code.astype(F32), 0.0).astype(BF16)
@@ -189,17 +226,24 @@
     values = weights * pick(origin, surface)
     sb[:, 0:ROWS, :] = values.reshape(n_gi, ROWS, cols)
     sb[:, ROWS:MSG, :] = targets.reshape(n_gi, 8, cols)
-    to_grp = jnp.where(is_ocean, RELAY, ocean_g)
-    my_slot = jnp.where(is_ocean, gi, g * n_gi + gi)
-    first = [
-        pltpu.make_async_remote_copy(
+    def first(q):
+        to_grp = jnp.where(is_ocean, RELAY, collector(q))
+        return pltpu.make_async_remote_copy(
             src_ref=sb.at[q], dst_ref=rb.at[my_slot], send_sem=sem_p1_s.at[q],
             recv_sem=sem_p1_r.at[my_slot], device_id=(to_grp, q * NZ + z), device_id_type=MESH,
         )
-        for q in range(n_gi)
-    ]
+
+    def own_first(q):
+        return pltpu.make_async_copy(sb.at[q], rb.at[my_slot], sem_p1_r.at[my_slot])
+
+    def is_own(q):
+        return jnp.logical_and(is_near, gi == q)
+
     pl.semaphore_wait(barrier, greetings)
-    for c in first + counts + halo:
+    for q in range(n_gi):
+        pl.when(is_own(q))(lambda q=q: own_first(q).start())
+        pl.when(jnp.logical_not(is_own(q)))(lambda q=q: first(q).start())
+    for c in counts + halo:
         c.start()
 
     for c in loads[6:]:
@@ -251,16 +295,25 @@
         ).wait_recv()
 
     def dense(rows, ids, height):
-        return pick((iota((height, lanes), 0) == ids).astype(BF16), rows)
+        return pick((iota((height, ids.shape[1]), 0) == ids).astype(BF16), rows)
 
     def second(make):
         return [make(r, gi * NZ + lax.rem(z + r, NZ)) for r in range(1, NZ)]
 
     def ocean_copy(r, dd):
         return pltpu.make_async_remote_copy(
-            src_ref=db.at[lax.rem(z + r, NZ)], dst_ref=ob.at[z], send_sem=sem_p2_s.at[r, 0],
-            recv_sem=sem_p2_r.at[z, 0], device_id=(ocean_g, dd), device_id_type=MESH,
-        )
+            src_ref=db.at[lax.rem(z + r, NZ)], dst_ref=ob.at[NZ + z], send_sem=sem_p2_s.at[r, 0],
+            recv_sem=sem_p2_r.at[NZ + z, 0], device_id=(ocean_g, dd), device_id_type=MESH,
+        )
+
+    def near_copies():
+        return [
+            pltpu.make_async_remote_copy(
+                src_ref=db.at[r], dst_ref=ob.at[z], send_sem=sem_p2_s.at[r, 0],
+                recv_sem=sem_p2_r.at[z, 0], device_id=(ocean_g, gi * NZ + r), device_id_type=MESH,
+            )
+            for r in range(NZ)
+        ]
 
     def relay_rows(r, dd):
         zz = lax.rem(z + r, NZ)
@@ -277,19 +330,27 @@
             recv_sem=sem_p2_r.at[z, 1], device_id=(RELAY, dd), device_id_type=MESH,
         )
 
-    def ocean_second():
-        for s in range(ocean_g * n_gi):
+    def collect():
+        for s in range(n_in):
             received_wait(rb.at[s], sem_p1_r.at[s])
         for zz in range(NZ):
             total = jnp.zeros((blocks, cols), F32)
-            for gg in range(ocean_g):
-                sl = slice(gg * n_gi, (gg + 1) * n_gi)
-                rows = rb[sl, zz * CAP : (zz + 1) * CAP, :].reshape(lanes, cols)
-                ids = jnp.sum(rb[sl, ROWS:MSG, :], axis=0)[zz : zz + 1, 0:lanes].astype(jnp.int32)
-                total += dense(rows, ids, blocks)
+            for lo, hi in ((0, n_gi), (n_gi, n_in)):
+                width = (hi - lo) * CAP
+                rows = rb[lo:hi, zz * CAP : (zz + 1) * CAP, :].reshape(width, cols)
+                ids = jnp.sum(rb[lo:hi, ROWS:MSG, :], axis=0)[zz : zz + 1, 0:width]
+                total += dense(rows, ids.astype(jnp.int32), blocks)
             db[zz] = total
-        for c in second(ocean_copy):
-            c.start()
+
+        @pl.when(is_ocean)
+        def _():
+            for c in second(ocean_copy):
+                c.start()
+
+        @pl.when(is_near)
+        def _():
+            for c in near_copies():
+                c.start()
 
     def relay_second():
         for s in range(n_gi):
@@ -370,7 +431,7 @@
             out[b, f0 + 1] = res[2 * u + 1]
 
     def step(i, carry):
-        pl.when(jnp.logical_and(is_ocean, i == SECOND))(ocean_second)
+        pl.when(jnp.logical_and(jnp.logical_or(is_ocean, is_near), i == SECOND))(collect)
         pl.when(jnp.logical_and(is_relay, i == SECOND))(relay_second)
         pl.when(i == EARLY)(lambda: outer(0))
         mine = [RIM + i * UNIT + u for u in range(UNIT)]
@@ -397,8 +458,11 @@
         got = db[z]
         for r in range(1, NZ):
             zz = lax.rem(z + r, NZ)
-            received_wait(ob.at[zz], sem_p2_r.at[zz, 0])
-            got += ob[zz]
+            received_wait(ob.at[NZ + zz], sem_p2_r.at[NZ + zz, 0])
+            got += ob[NZ + zz]
+        for r in range(NZ):
+            received_wait(ob.at[r], sem_p2_r.at[r, 0])
+            got += ob[r]
         out[:, 0, 0, :] += got
         for c in second(ocean_copy):
             c.wait_send()
@@ -414,7 +478,14 @@
         received_wait(gb, sem_p3_r.at[0])
         out[:, 0, lev - 1, :] += gb[...]
 
-    for c in halo + counts + first:
+    @pl.when(is_near)
+    def _():
+        for c in near_copies():
+            c.wait_send()
+
+    for q in range(n_gi):
+        pl.when(jnp.logical_not(is_own(q)))(lambda q=q: first(q).wait_send())
+    for c in halo + counts:
         c.wait_send()
 
 
@@ -454,11 +525,11 @@
             vm((16, cols), F32),
             vm((16, cols), F32),
             vm((n_gi, MSG, cols), F32),
-            vm(((n_grp - 1) * n_gi, MSG, cols), F32),
+            vm(((n_grp - 1) * n_gi // 2, MSG, cols), F32),
             vm((NZ, n_gi, CAP, cols), F32),
             vm((NZ, n_gi, 8, cols), F32),
             vm((NZ, blocks, cols), F32),
-            vm((NZ, blocks, cols), F32),
+            vm((2 * NZ, blocks, cols), F32),
             vm((blocks, cols), F32),
             vm(((n_grp - 1) * blocks, cols), F32),
             dma((CHUNKS,)),
@@ -468,9 +539,9 @@
             dma((2,)),
             dma((2,)),
             dma((n_gi,)),
-            dma(((n_grp - 1) * n_gi,)),
+            dma(((n_grp - 1) * n_gi // 2,)),
             dma((NZ, 2)),
-            dma((NZ, 2)),
+            dma((2 * NZ, 2)),
             dma((n_grp - 2,)),
             dma((1,)),
         ],

time: 36.3 us -> 35.5 us (0.978)
  Pallas kernels: 32.4 us -> 31.6 us
    pallas_call x1, Pallas kernels: 32.4 us -> 31.6 us  [per_device(): call(state, neighbours.T, remap_dest.reshape(1, n_rows), remap_src.reshap...]
where the time goes in v4:
time: 35.5 us; the launch traced here: 35.4 us
  Pallas kernels  31.6 us (89%)
  local copies, waits for them, and re-layouts  3.74 us (11%)
    pallas_call x1, Pallas kernels, per_device(): call(state, neighbours.T, remap_dest.reshape(1, n_rows), remap_src.reshap...  31.6 us
    unnamed x1, local copies, waits for them, and re-layouts  3.74 us

profile of v4, /device:TPU:1, one launch (start us, length us, event | category | flops | bytes accessed | tf_op | source)
XLA Modules:
  0.0 35.4 jit_solution(3161760276657923926)
XLA Ops:
  0.0 31.6 %interval.1 = f32[64,4,72,128]{3,2,1,0:T(8,128)S(1)} custom-call(f32[64,4,72,128]{3,2,1,0:T(8,128)} %state.1, s32[4,64]{1,0:T(4,128)} %bitcast.4, s32[1,512]{1,0:T(1,128)} %bitcast.5, s32[1,512]{1,0:T(1,128)} %bitcast.6, s32[1,512]{1,0:T(1,128)} %bitcast.7, f32[512,128]{1,0:T(8,128)} %wts_in.1, f32[2,128,128]{2,1,0:T(8,128)} %self_in.1, ...), custom_call_target="tpu_custom_call" | custom-call | tf_op jit(solution)/shard_map/interval/pallas_call | solution.py:553
  31.6 3.7 %copy.11 = f32[64,4,72,128]{3,2,1,0:T(8,128)} copy(f32[64,4,72,128]{3,2,1,0:T(8,128)S(1)} %interval.1) | data formatting | bytes 18874368

commit v5 on v4

--- a/solution.py
+++ b/solution.py
@@ -431,7 +431,6 @@
             out[b, f0 + 1] = res[2 * u + 1]
 
     def step(i, carry):
-        pl.when(jnp.logical_and(jnp.logical_or(is_ocean, is_near), i == SECOND))(collect)
         pl.when(jnp.logical_and(is_relay, i == SECOND))(relay_second)
         pl.when(i == EARLY)(lambda: outer(0))
         mine = [RIM + i * UNIT + u for u in range(UNIT)]
@@ -450,6 +449,7 @@
         return carry
 
     lax.fori_loop(0, (blocks - 2 * RIM) // UNIT, step, 0)
+    pl.when(jnp.logical_or(is_ocean, is_near))(collect)
     outer(2)
     pl.when(is_relay)(relay_third)
 

time: 35.5 us -> 35.5 us (level)
  no operation moved by 1% of the time
where the time goes in v5:
time: 35.5 us; the launch traced here: 35.3 us
  Pallas kernels  31.6 us (89%)
  local copies, waits for them, and re-layouts  3.74 us (11%)
    pallas_call x1, Pallas kernels, per_device(): call(state, neighbours.T, remap_dest.reshape(1, n_rows), remap_src.reshap...  31.6 us
    unnamed x1, local copies, waits for them, and re-layouts  3.74 us

profile of v5, /device:TPU:1, one launch (start us, length us, event | category | flops | bytes accessed | tf_op | source)
XLA Modules:
  0.0 35.3 jit_solution(8134529057056587263)
XLA Ops:
  0.0 31.6 %interval.1 = f32[64,4,72,128]{3,2,1,0:T(8,128)S(1)} custom-call(f32[64,4,72,128]{3,2,1,0:T(8,128)} %state.1, s32[4,64]{1,0:T(4,128)} %bitcast.4, s32[1,512]{1,0:T(1,128)} %bitcast.5, s32[1,512]{1,0:T(1,128)} %bitcast.6, s32[1,512]{1,0:T(1,128)} %bitcast.7, f32[512,128]{1,0:T(8,128)} %wts_in.1, f32[2,128,128]{2,1,0:T(8,128)} %self_in.1, ...), custom_call_target="tpu_custom_call" | custom-call | tf_op jit(solution)/shard_map/interval/pallas_call | solution.py:553
  31.6 3.7 %copy.11 = f32[64,4,72,128]{3,2,1,0:T(8,128)} copy(f32[64,4,72,128]{3,2,1,0:T(8,128)S(1)} %interval.1) | data formatting | bytes 18874368
